TPU v7x, 256 devices: a whole 4x4x8 slice. The times are simulated.
256 devices in a mesh: ctx: 32 (over y, x, core), kvh: 8 (over z).
Axes of the slice: x: 4, y: 4, z: 8, core: 2. Of those that a mesh axis runs over, the one named last changes fastest.
Arguments:
- hidden_in: bfloat16 [4, 8192], P(None, 'ctx'), may hold values from -6 to 6
- w_query: bfloat16 [8192, 8192], P('ctx', 'kvh'), may hold values from -0.0625 to 0.0625
- key_cache: bfloat16 [768, 512, 1024], P('ctx', None, 'kvh')
- value_cache: bfloat16 [768, 512, 1024], P('ctx', None, 'kvh'), may hold values from -6 to 6
- chosen: int32 [4, 8, 16], P(None, 'kvh'), may hold values from 0 to 191, all different within a row
- owner_map: int32 [768], replicated, may hold values from 0 to 767, each once
- w_out: bfloat16 [8192, 8192], P('kvh', 'ctx'), may hold values from -0.75 to 0.75
Outputs:
- mixed: bfloat16 [4, 8192], P(None, ('ctx', 'kvh'))
Inputs may be any that keep to these rules, and one draw needn't show every extreme that they name: `chosen`: distinct within a request and KV head. `owner_map`: A permutation; the block at storage position p lies on index p // 24 of ctx, in its slot p % 24.
All inputs are finite; a program needn't handle non-finite values.
Results may differ from a plain program's by a relative error of at most 0.012.
Values may be sent and summed in bfloat16 or wider, within the bound.
No kernel may reach another device: no remote copies, remote signals or barrier semaphores. Data moves between devices by JAX's collectives and lax.ppermute only.
A program may use at most 64 MiB of HBM per device.

v0:
```python
import jax
import jax.numpy as jnp
from jax import lax
from jax.sharding import PartitionSpec as P

QPK = 8
HD = 128


def combined_all(part, axis, combine):
    gathered = jax.tree.map(lambda a: lax.all_gather(a, axis), part)

    def take(source):
        return jax.tree.map(lambda a: lax.dynamic_index_in_dim(a, source, 0, False), gathered)

    return lax.fori_loop(
        1, lax.axis_size(axis), lambda source, state: combine(state, take(source)), take(0)
    )


def block_partial(query_rows, key_block, value_block):
    scores = jnp.dot(query_rows, key_block.T, preferred_element_type=jnp.float32) / jnp.sqrt(
        jnp.float32(HD)
    )
    peak = jnp.max(scores, axis=-1)
    expo = jnp.exp(scores - peak[:, None])
    total = jnp.sum(expo, axis=-1)
    weights = expo.astype(jnp.bfloat16)
    out = jnp.dot(weights, value_block, preferred_element_type=jnp.float32)
    return (peak, total, out)


def join_states(first, second):
    peak_a, total_a, acc_a = first
    peak_b, total_b, acc_b = second
    peak_new = jnp.maximum(peak_a, peak_b)
    factor_a = jnp.exp(peak_a - peak_new)
    factor_b = jnp.exp(peak_b - peak_new)
    total_new = total_a * factor_a + total_b * factor_b
    acc_new = acc_a * factor_a[..., None] + acc_b * factor_b[..., None]
    return (peak_new, total_new, acc_new)


def local(hidden_in, w_query, key_cache, value_cache, chosen, owner_map, w_out):
    nreq = hidden_in.shape[0]
    heads_local = chosen.shape[1]
    topb = chosen.shape[2]
    blk_dev = key_cache.shape[0]
    block = key_cache.shape[1]
    head_dim = HD
    group = QPK
    nblk = owner_map.shape[0] // nreq
    columns = heads_local * group * head_dim
    partial_query = jnp.dot(hidden_in, w_query, preferred_element_type=jnp.float32)
    query = lax.psum(partial_query, "ctx").astype(jnp.bfloat16)
    query = query.reshape(nreq, heads_local, group, head_dim)
    me_ctx = lax.axis_index("ctx")
    items = nreq * heads_local * topb
    counter = jnp.arange(items, dtype=jnp.int32)
    req_id = counter // (heads_local * topb)
    head_id = counter // topb % heads_local
    glob = req_id * nblk + chosen.reshape(items)
    table_ids = jnp.arange(owner_map.shape[0], dtype=jnp.int32)
    position = jnp.sum(
        jnp.where(glob[:, None] == table_ids[None, :], owner_map[None, :], 0), axis=1
    )
    is_local = position // blk_dev == me_ctx
    slot_id = position % blk_dev
    count = jnp.sum(is_local.astype(jnp.int32))
    order = jnp.argsort(jnp.where(is_local, 0, 1).astype(jnp.int32), stable=True)
    peak0 = jnp.full((nreq, heads_local, group), -1e30, jnp.float32)
    total0 = jnp.zeros((nreq, heads_local, group), jnp.float32)
    acc0 = jnp.zeros((nreq, heads_local, group, head_dim), jnp.float32)

    def visit(step_index, state):
        peak_all, total_all, acc_all = state
        item = order[step_index]
        req = req_id[item]
        head = head_id[item]
        slot = slot_id[item]
        zero = jnp.int32(0)
        key_block = lax.dynamic_slice(
            key_cache, (slot, zero, head * head_dim), (1, block, head_dim)
        )[0]
        value_block = lax.dynamic_slice(
            value_cache, (slot, zero, head * head_dim), (1, block, head_dim)
        )[0]
        query_rows = lax.dynamic_slice(
            query, (req, head, zero, zero), (1, 1, group, head_dim)
        ).reshape(group, head_dim)
        peak_b, total_b, out_b = block_partial(query_rows, key_block, value_block)
        old_peak = lax.dynamic_slice(peak_all, (req, head, zero), (1, 1, group)).reshape(group)
        old_total = lax.dynamic_slice(total_all, (req, head, zero), (1, 1, group)).reshape(group)
        old_acc = lax.dynamic_slice(
            acc_all, (req, head, zero, zero), (1, 1, group, head_dim)
        ).reshape(group, head_dim)
        new_peak, new_total, new_acc = join_states(
            (old_peak, old_total, old_acc), (peak_b, total_b, out_b)
        )
        peak_all = lax.dynamic_update_slice(
            peak_all, new_peak.reshape(1, 1, group), (req, head, zero)
        )
        total_all = lax.dynamic_update_slice(
            total_all, new_total.reshape(1, 1, group), (req, head, zero)
        )
        acc_all = lax.dynamic_update_slice(
            acc_all, new_acc.reshape(1, 1, group, head_dim), (req, head, zero, zero)
        )
        return (peak_all, total_all, acc_all)

    peak_loc, total_loc, acc_loc = lax.fori_loop(jnp.int32(0), count, visit, (peak0, total0, acc0))
    peak_all, total_all, acc_all = combined_all((peak_loc, total_loc, acc_loc), "ctx", join_states)
    attn = (acc_all / total_all[..., None]).reshape(nreq, columns).astype(jnp.bfloat16)
    term = jnp.dot(attn, w_out, preferred_element_type=jnp.float32)
    return lax.psum_scatter(term, "kvh", scatter_dimension=1, tiled=True).astype(jnp.bfloat16)


def solution(mesh):
    placed = (
        P(None, "ctx"),
        P("ctx", "kvh"),
        P("ctx", None, "kvh"),
        P("ctx", None, "kvh"),
        P(None, "kvh", None),
        P(),
        P("kvh", "ctx"),
    )
    return jax.shard_map(
        local, mesh=mesh, in_specs=placed, out_specs=P(None, ("ctx", "kvh")), check_vma=False
    )
```

profile of v0, /device:TPU:4, one launch (start us, length us, event | category | flops | bytes accessed | tf_op | source)
XLA Modules:
  0.0 330.8 jit_solution(4014002742601760562)
XLA Ops:
  7.1 1.4 reduce.3
  8.6 0.9 select_reduce_fusion
  9.5 0.7 fusion.28
  10.2 0.9 fusion.30
  11.1 118.3 %psum.7 = bf16[4,1024]{1,0:T(4,128)(2,1)S(1)} all-reduce(f32[4,1024]{1,0:T(4,128)S(1)} %fusion.30), channel_id=1, replica_groups=mesh['ctx'=32,'kvh'=8] {'ctx'}, use_global_device_ids=true, to_apply=%region_3.4 | all-reduce | flops 4096 | bytes 24576 | tf_op jit(solution)/shard_map/psum | solution.py:55
  129.4 2.1 sort.17
  131.5 33.2 %while.34 = (s32[]{:T(128)}, f32[4,1,8]{2,1,0:T(1,128)S(1)}, f32[4,1,8]{2,1,0:T(1,128)S(1)}, f32[4,1,8,128]{3,2,1,0:T(8,128)S(1)}, s32[]{:T(128)}, /*index=5*/s3...) while((s32[]{:T(128)}, f32[4,1,8]{2,1,0:T(1,128)S(1)}, ...), condition=%wide.region_7.8_spmd, body=%wide.region_4.7_spmd.sunk | while | flops 2124878 | bytes 335013 | solution.py:111
  132.2 0.6 dynamic_slice.137
  137.2 0.6 dynamic_slice.139
  139.8 1.2 fusion.46
  141.2 1.1 fusion.50
  148.0 0.6 dynamic_slice.139
  150.6 1.2 fusion.46
  152.0 1.1 fusion.50
  158.9 0.6 dynamic_slice.139
  161.4 1.2 fusion.46
  162.8 1.1 fusion.50
  164.6 40.5 %all-gather = f32[128,1,8]{2,1,0:T(1,128)S(1)} all-gather(f32[4,1,8]{2,1,0:T(1,128)S(1)} %get-tuple-element.271), channel_id=2, replica_groups=mesh['ctx'=32,'kvh'=8] {'ctx'}, dimensions={0}, use_global_device_ids=true | all-gather | bytes 4224 | tf_op jit(solution)/shard_map/all_gather | solution.py:11
  205.2 24.3 %all-gather.1 = f32[128,1,8]{2,1,0:T(1,128)S(1)} all-gather(f32[4,1,8]{2,1,0:T(1,128)S(1)} %get-tuple-element.272), channel_id=3, replica_groups=mesh['ctx'=32,'kvh'=8] {'ctx'}, dimensions={0}, use_global_device_ids=true | all-gather | bytes 4224 | tf_op jit(solution)/shard_map/all_gather | solution.py:11
  229.4 22.1 %all-gather.2 = f32[128,1,8,128]{3,2,1,0:T(8,128)S(1)} all-gather(f32[4,1,8,128]{3,2,1,0:T(8,128)S(1)} %get-tuple-element.273), channel_id=4, replica_groups=mesh['ctx'=32,'kvh'=8] {'ctx'}, dimensions={0}, use_global_device_ids=true | all-gather | bytes 540672 | tf_op jit(solution)/shard_map/all_gather | solution.py:11
  251.5 3.9 %while.35 = (s32[]{:T(128)}, f32[4,1,8]{2,0,1:T(4,128)S(1)}, f32[4,1,8]{2,0,1:T(4,128)S(1)}, f32[4,1,8,128]{3,2,1,0:T(8,128)S(1)}, f32[32,4,1,8]{3,1,2,0:T(4,128...) while((s32[]{:T(128)}, f32[4,1,8]{2,0,1:T(4,128)S(1)}, ...), condition=%wide.region_9.10_spmd, body=%wide.region_8.9_spmd.sunk | while | flops 12517 | bytes 51219 | solution.py:16
  255.4 1.0 convolution_bitcast_fusion
  256.5 66.2 %reduce-scatter.4.cloned.1.call-done = f32[32,4]{1,0:T(8,128)} async-done(((f32[256,4]{1,0:T(8,128)}), f32[32,4]{1,0:T(8,128)}) %reduce-scatter.4.cloned.1.call-update) | async-done | bytes 528
  322.6 1.4 copy.24
  (163 shorter events, 8.1 us)
Async XLA Ops:
  6.5 3.7 %copy-start = (bf16[256,1024]{1,0:T(8,128)(2,1)S(1)}, bf16[256,1024]{1,0:T(8,128)(2,1)}, u32[]{:S(2)}) copy-start(bf16[256,1024]{1,0:T(8,128)(2,1)} %param.12) | copy-start | bytes 1572868
  6.5 248.9 %copy-start.1 = (bf16[1024,256]{1,0:T(8,128)(2,1)S(1)}, bf16[1024,256]{1,0:T(8,128)(2,1)}, u32[]{:S(2)}) copy-start(bf16[1024,256]{1,0:T(8,128)(2,1)} %param.17) | copy-start | bytes 1572868
  6.5 316.1 %reduce-scatter.4.cloned.1.call-start = ((), (), s32[]{:S(2)}) async-start(), calls=%async_computation.1 | async-start | bytes 147456
Sparse Core Ops, SparseCore 0:
  256.6 65.9 reduce-scatter.3
where the time goes:
time: 332 us; the launch traced here: 331 us
  blocking collectives  205 us (62%)
  waiting for transfers between devices  66.2 us (20%)
  loops' own time  20.5 us (6%)
  between operations  13.4 us (4%)
  other arithmetic  9.28 us (3%)
  matrix products  8.64 us (3%)
  local copies, waits for them, and re-layouts  7.7 us (2%)
    psum x1, blocking collectives, local(): query = lax.psum(partial_query, 'ctx').astype(jnp.bfloat16)  118 us
    all_gather x3, blocking collectives, combined_all(): gathered = jax.tree.map(lambda a: lax.all_gather(a, axis), part)  86.9 us
    unnamed x2, waiting for transfers between devices  66.2 us
    another operation x1, loops' own time, local(): lax.fori_loop(jnp.int32(0), count, visit, (peak0, total0, acc0))  20.1 us
  transfers between devices with their start and end apart: 1, of which 1 were waited for; matrix products, arithmetic and copies ran while one was open for 0% of the time, Pallas kernels for 0%

commit v1 on v0

v1 whole, which is shorter than its diff:
```python
import functools

import jax
import jax.numpy as jnp
from jax import lax
from jax.experimental import pallas as pl
from jax.experimental.pallas import tpu as pltpu
from jax.sharding import PartitionSpec as P

QPK = 8
HD = 128
NEG = -1e30
VMEM = pl.BlockSpec(memory_space=pltpu.VMEM)
SMEM = pl.BlockSpec(memory_space=pltpu.SMEM)
ANY = pl.BlockSpec(memory_space=pl.ANY)
HBM = pl.BlockSpec(memory_space=pltpu.HBM)
LIMIT = 24 * 1024 * 1024
GROUP = 4
AHEAD = 8
CTX_FIRST = 21
KVH_FIRST = 4


def in_hbm(array):
    return pltpu.with_memory_space_constraint(array, pltpu.HBM)


def query_kernel(
    hidden_ref, weight_ref, send_ref, keep_ref, hidden, weight, rows_ref, hidden_sem, weight_sem
):
    copies = (
        pltpu.make_async_copy(hidden_ref, hidden, hidden_sem),
        pltpu.make_async_copy(weight_ref, weight, weight_sem),
    )
    for copy in copies:
        copy.start()
    for copy in copies:
        copy.wait()
    part = jnp.dot(hidden[...], weight[...], preferred_element_type=jnp.float32)
    nreq = part.shape[0]
    for g in range(QPK):
        rows_ref[pl.ds(g, nreq, stride=QPK), :] = part[:, g * HD : (g + 1) * HD]
    half = keep_ref.shape[0]
    core = lax.rem(lax.axis_index("ctx"), 2)
    keep_ref[...] = rows_ref[pl.ds(pl.multiple_of(core * half, half), half), :]
    send_ref[...] = rows_ref[pl.ds(pl.multiple_of((1 - core) * half, half), half), :]


def spread_kernel(keep_ref, swapped_ref, out_ref):
    pair = keep_ref[...] + swapped_ref[...]
    for d in range(out_ref.shape[0]):
        out_ref[d] = pair


def fetch_kernel(
    chosen_ref, owner_ref, key_ref, value_ref, after_ref, key_buf, value_buf, items_ref,
    chosen, owner, sems, key_sem, value_sem,
):
    del after_ref
    slots_here = key_ref.shape[0]
    ahead = key_buf.shape[0]
    nreq, _, topb = chosen_ref.shape
    nblk = owner_ref.shape[0] // nreq
    last = items_ref.shape[0] - 1
    first = lax.axis_index("ctx") * slots_here
    tables = (
        pltpu.make_async_copy(chosen_ref, chosen, sems.at[0]),
        pltpu.make_async_copy(owner_ref, owner, sems.at[1]),
    )
    for copy in tables:
        copy.start()
    for copy in tables:
        copy.wait()

    def copies(place):
        slot = items_ref[slots_here + place]
        return (
            pltpu.make_async_copy(key_ref.at[slot], key_buf.at[place], key_sem.at[place]),
            pltpu.make_async_copy(value_ref.at[slot], value_buf.at[place], value_sem.at[place]),
        )

    for i in range(slots_here + GROUP):
        items_ref[i] = 0
    count = jnp.int32(0)
    for r in range(nreq):

        def look(j, count):
            slot = owner[r * nblk + chosen[r, 0, j]] - first
            here = (slot >= 0) & (slot < slots_here)

            @pl.when(here)
            def _():
                items_ref[count] = r
                items_ref[slots_here + count] = slot

            @pl.when(here & (count < ahead))
            def _():
                for copy in copies(count):
                    copy.start()

            return count + here.astype(jnp.int32)

        count = lax.fori_loop(0, topb, look, count, unroll=4)
    items_ref[last] = count

    def arrive(i, carry):
        for copy in copies(i):
            copy.wait()
        return carry

    lax.fori_loop(0, jnp.minimum(count, ahead), arrive, 0)


def attend_kernel(
    parts_ref, items_ref, key_ref, value_ref, key_all, value_all, out_ref,
    query_ref, top_ref, total_ref, acc_ref, key_late, value_late, key_sem, value_sem,
):
    slots_here = key_all.shape[0]
    ahead = key_ref.shape[0]
    count = items_ref[items_ref.shape[0] - 1]

    def copies(i):
        place, slot = i - ahead, items_ref[slots_here + i]
        return (
            pltpu.make_async_copy(key_all.at[slot], key_late.at[place], key_sem.at[place]),
            pltpu.make_async_copy(value_all.at[slot], value_late.at[place], value_sem.at[place]),
        )

    def bring(i, carry):
        for copy in copies(i):
            copy.start()
        return carry

    def arrive(i, carry):
        for copy in copies(i):
            copy.wait()
        return carry

    lax.fori_loop(ahead, count, bring, 0)
    half = parts_ref.shape[1]
    for side in range(2):
        query = parts_ref[1 - side]
        for d in range(side + 2, parts_ref.shape[0], 2):
            query = query + parts_ref[d]
        query_ref[side * half : (side + 1) * half, :] = query
    top_ref[...] = jnp.full(top_ref.shape, NEG, jnp.float32)
    total_ref[...] = jnp.zeros(total_ref.shape, jnp.float32)
    acc_ref[...] = jnp.zeros(acc_ref.shape, jnp.float32)

    def visit(step, keys, values, base):
        found = []
        for u in range(GROUP):
            place = step * GROUP + u
            i = base + place
            rows = pl.ds(pl.multiple_of(items_ref[i] * QPK, QPK), QPK)
            scores = lax.dot_general(
                query_ref[rows, :].astype(jnp.bfloat16), keys[place], (((1,), (1,)), ((), ())),
                preferred_element_type=jnp.float32,
            ) * (1.0 / HD**0.5)
            peak = jnp.max(scores, axis=1, keepdims=True)
            expo = jnp.exp(scores - peak)
            total = jnp.sum(expo, axis=1, keepdims=True)
            out = jnp.dot(
                expo.astype(jnp.bfloat16), values[place], preferred_element_type=jnp.float32
            )
            found.append((i < count, rows, peak, total, out))
        for here, rows, peak, total, out in found:
            peak = jnp.where(here, peak, NEG)
            old = top_ref[rows, :]
            new = jnp.maximum(old, peak)
            keep = jnp.exp(old - new)
            add = jnp.where(here, jnp.exp(peak - new), 0.0)
            top_ref[rows, :] = new
            total_ref[rows, :] = total_ref[rows, :] * keep + jnp.where(here, total, 0.0) * add
            acc_ref[rows, :] = acc_ref[rows, :] * keep + jnp.where(here, out, 0.0) * add

    for step in range(ahead // GROUP):

        @pl.when(step * GROUP < count)
        def _():
            visit(step, key_ref, value_ref, 0)

    lax.fori_loop(ahead, count, arrive, 0)

    def visit_late(step, carry):
        visit(step, key_late, value_late, ahead)
        return carry

    lax.fori_loop(0, jnp.maximum(count - ahead + GROUP - 1, 0) // GROUP, visit_late, 0)

    total = total_ref[...]
    some = total > 0.0
    safe = jnp.where(some, total, 1.0)
    mean = (acc_ref[...] / safe).astype(jnp.bfloat16)
    level = jnp.where(some, top_ref[...] + jnp.log(safe), NEG)
    high = level.astype(jnp.bfloat16).astype(jnp.float32)
    middle = (level - high).astype(jnp.bfloat16).astype(jnp.float32)
    low = level - high - middle
    nrow = level.shape[0]
    lane = lax.broadcasted_iota(jnp.int32, level.shape, 1)
    row = lax.broadcasted_iota(jnp.int32, level.shape, 0)
    packed = jnp.where(lane == row, high, 0.0)
    packed = jnp.where(lane == row + nrow, middle, packed)
    packed = jnp.where(lane == row + 2 * nrow, low, packed)
    packed = jnp.sum(packed, axis=0, keepdims=True)
    packed = jnp.broadcast_to(packed, (out_ref.shape[1] - nrow, HD)).astype(jnp.bfloat16)
    for d in range(out_ref.shape[0]):
        out_ref[d, :nrow, :] = mean
        out_ref[d, nrow:, :] = packed


def project_kernel(parts_ref, weight_ref, out_ref, level_ref, rows_ref):
    ndev = parts_ref.shape[0]
    nrow = rows_ref.shape[0]
    lane = lax.broadcasted_iota(jnp.int32, (nrow, HD), 1)
    row = lax.broadcasted_iota(jnp.int32, (nrow, HD), 0)
    mine = (lane == row) | (lane == row + nrow) | (lane == row + 2 * nrow)
    top = jnp.full((nrow, 1), NEG, jnp.float32)
    for d in range(ndev):
        packed = parts_ref[d, nrow:, :].astype(jnp.float32)[:1]
        level = jnp.sum(jnp.where(mine, packed, 0.0), axis=1, keepdims=True)
        level_ref[d] = jnp.broadcast_to(level, (nrow, HD))
        top = jnp.maximum(top, level)
    total = jnp.zeros((nrow, HD), jnp.float32)
    acc = jnp.zeros((nrow, HD), jnp.float32)
    for d in range(ndev):
        share = jnp.exp(level_ref[d] - top)
        total = total + share
        acc = acc + share * parts_ref[d, :nrow, :].astype(jnp.float32)
    rows_ref[...] = acc / total
    nreq = nrow // QPK
    term = jnp.zeros((nreq, weight_ref.shape[1]), jnp.float32)
    for g in range(QPK):
        heads = rows_ref[pl.ds(g, nreq, stride=QPK), :].astype(jnp.bfloat16)
        term = term + jnp.dot(
            heads, weight_ref[g * HD : (g + 1) * HD, :], preferred_element_type=jnp.float32
        )
    ndest = out_ref.shape[0]
    width = weight_ref.shape[1] // ndest
    for k in range(ndest):
        out_ref[(k - KVH_FIRST) % ndest, :, :width] = term[:, k * width : (k + 1) * width]


def sum_kernel(terms_ref, out_ref):
    out_ref[...] = jnp.sum(terms_ref[...], axis=0)[:, : out_ref.shape[1]].astype(out_ref.dtype)


def order(n, first):
    return [[first, first ^ 1] + [i for i in range(n) if i // 2 != first // 2]]


def turned(n, first):
    return [[(first + i) % n for i in range(n)]]


def local(nctx, nkvh, hidden_in, w_query, key_cache, value_cache, chosen, owner_map, w_out):
    nreq = hidden_in.shape[0]
    nrow = nreq * QPK
    slots_here, block, _ = key_cache.shape
    params = pltpu.CompilerParams(vmem_limit_bytes=LIMIT)
    state = pltpu.VMEM((nrow, HD), jnp.float32)
    half = jax.ShapeDtypeStruct((nrow // 2, HD), jnp.float32)
    send, keep = pl.pallas_call(
        query_kernel,
        out_shape=(half, half),
        in_specs=[HBM, HBM],
        out_specs=(VMEM, VMEM),
        scratch_shapes=[
            pltpu.VMEM(hidden_in.shape, hidden_in.dtype),
            pltpu.VMEM(w_query.shape, w_query.dtype),
            state,
            pltpu.SemaphoreType.DMA,
            pltpu.SemaphoreType.DMA,
        ],
        compiler_params=params,
        name="query",
    )(in_hbm(hidden_in), in_hbm(w_query))
    swapped = lax.ppermute(send, "ctx", [(i, i ^ 1) for i in range(nctx)])
    parts = pl.pallas_call(
        spread_kernel,
        out_shape=pltpu.VMEM((nctx, nrow // 2, HD), jnp.float32),
        in_specs=[VMEM, VMEM],
        out_specs=VMEM,
        compiler_params=params,
        name="spread",
    )(keep, swapped)
    every = lax.all_to_all(parts, "ctx", 0, 0, tiled=True, axis_index_groups=order(nctx, CTX_FIRST))
    blocks = pltpu.VMEM((AHEAD, block, HD), key_cache.dtype)
    late = slots_here - AHEAD
    keys, values, items = pl.pallas_call(
        fetch_kernel,
        out_shape=(blocks, blocks, jax.ShapeDtypeStruct((2 * slots_here + 8,), jnp.int32)),
        in_specs=[HBM, HBM, HBM, HBM, ANY],
        out_specs=(VMEM, VMEM, SMEM),
        scratch_shapes=[
            pltpu.SMEM(chosen.shape, jnp.int32),
            pltpu.SMEM(owner_map.shape, jnp.int32),
            pltpu.SemaphoreType.DMA((2,)),
            pltpu.SemaphoreType.DMA((AHEAD,)),
            pltpu.SemaphoreType.DMA((AHEAD,)),
        ],
        compiler_params=params,
        cost_estimate=pl.CostEstimate(flops=0, transcendentals=0, bytes_accessed=8 << 20),
        name="fetch",
    )(in_hbm(chosen), in_hbm(owner_map), in_hbm(key_cache), in_hbm(value_cache), swapped)
    means = pl.pallas_call(
        attend_kernel,
        out_shape=jax.ShapeDtypeStruct((nctx, nrow + 16, HD), jnp.bfloat16),
        in_specs=[VMEM, SMEM, VMEM, VMEM, HBM, HBM],
        out_specs=VMEM,
        scratch_shapes=[
            state, state, state, state,
            pltpu.VMEM((late, block, HD), key_cache.dtype),
            pltpu.VMEM((late, block, HD), key_cache.dtype),
            pltpu.SemaphoreType.DMA((late,)),
            pltpu.SemaphoreType.DMA((late,)),
        ],
        compiler_params=params,
        name="attend",
    )(every, items, keys, values, in_hbm(key_cache), in_hbm(value_cache))
    means = lax.all_to_all(means, "ctx", 0, 0, tiled=True, axis_index_groups=order(nctx, CTX_FIRST))
    terms = pl.pallas_call(
        project_kernel,
        out_shape=jax.ShapeDtypeStruct((nkvh, nreq, HD), jnp.float32),
        in_specs=[VMEM, VMEM],
        out_specs=VMEM,
        scratch_shapes=[pltpu.VMEM((nctx, nrow, HD), jnp.float32), state],
        compiler_params=params,
        name="project",
    )(means, w_out)
    terms = lax.all_to_all(terms, "kvh", 0, 0, tiled=True, axis_index_groups=turned(nkvh, KVH_FIRST))
    return pl.pallas_call(
        sum_kernel,
        out_shape=jax.ShapeDtypeStruct((nreq, w_out.shape[1] // nkvh), jnp.bfloat16),
        in_specs=[VMEM],
        out_specs=VMEM,
        compiler_params=params,
        name="sum",
    )(terms)


def solution(mesh):
    placed = (
        P(None, "ctx"),
        P("ctx", "kvh"),
        P("ctx", None, "kvh"),
        P("ctx", None, "kvh"),
        P(None, "kvh", None),
        P(),
        P("kvh", "ctx"),
    )
    return jax.shard_map(
        functools.partial(local, mesh.shape["ctx"], mesh.shape["kvh"]),
        mesh=mesh, in_specs=placed, out_specs=P(None, ("ctx", "kvh")), check_vma=False,
    )
```

time: 332 us -> 45.9 us (0.14)
  blocking collectives: 205 us -> 26.3 us
  waiting for transfers between devices: 66.2 us -> 4.75 us
  loops' own time: 20.5 us -> 0 us
  between operations: 13.4 us -> 0.04 us
  other arithmetic: 9.28 us -> 0 us
  matrix products: 8.64 us -> 0 us
  Pallas kernels: 0 us -> 7.84 us
  local copies, waits for them, and re-layouts: 7.7 us -> 0.01 us
  starting transfers between devices: 0.01 us -> 6.61 us
    psum x1 -> x0, blocking collectives: 118 us -> none  [local(): query = lax.psum(partial_query, 'ctx').astype(jnp.bfloat16)]
    all_gather x3 -> x0, blocking collectives: 86.9 us -> none  [combined_all(): gathered = jax.tree.map(lambda a: lax.all_gather(a, axis), part)]
    unnamed x2 -> x0, waiting for transfers between devices: 66.2 us -> none
    all_to_all x0 -> x2, blocking collectives: none -> 26.3 us  [the longest x1 13.8 us: local(): lax.all_to_all(means, 'ctx', 0, 0, tiled=True, axis_index_groups=order(nc...]
    another operation x2 -> x0, loops' own time: 20.5 us -> none  [the longest x1 20.1 us: local(): lax.fori_loop(jnp.int32(0), count, visit, (peak0, total0, acc0))]
    pallas_call x0 -> x6, Pallas kernels: none -> 7.84 us  [the longest x1 2.76 us: local(): pl.pallas_call(fetch_kernel, out_shape=(blocks, blocks, jax.ShapeDtypeStr...]
    dot_general x7 -> x0, matrix products: 7.65 us -> none  [the longest x3 3.48 us: block_partial(): jnp.dot(query_rows, key_block.T, preferred_element_type=jnp.float32)]
    all_to_all x0 -> x1, starting transfers between devices: none -> 6.52 us  [local(): lax.all_to_all(parts, 'ctx', 0, 0, tiled=True, axis_index_groups=order(nc...]
  transfers between devices with their start and end apart: 1 -> 2, of which waited for: 1 -> 2; matrix products, arithmetic and copies ran while one was open for 0% -> 0% of each run, Pallas kernels for 0% -> 6%
where the time goes in v1:
time: 45.9 us; the launch traced here: 45.6 us
  blocking collectives  26.3 us (57%)
  Pallas kernels  7.84 us (17%)
  starting transfers between devices  6.61 us (14%)
  waiting for transfers between devices  4.75 us (10%)
    all_to_all x1, blocking collectives, local(): lax.all_to_all(means, 'ctx', 0, 0, tiled=True, axis_index_groups=order(nc...  13.8 us
    all_to_all x1, blocking collectives, local(): lax.all_to_all(terms, 'kvh', 0, 0, tiled=True, axis_index_groups=turned(n...  12.5 us
    all_to_all x1, starting transfers between devices, local(): lax.all_to_all(parts, 'ctx', 0, 0, tiled=True, axis_index_groups=order(nc...  6.52 us
    all_to_all x1, waiting for transfers between devices, local(): lax.all_to_all(parts, 'ctx', 0, 0, tiled=True, axis_index_groups=order(nc...  3.59 us
    pallas_call x1, Pallas kernels, local(): pl.pallas_call(fetch_kernel, out_shape=(blocks, blocks, jax.ShapeDtypeStr...  2.76 us
    pallas_call x1, Pallas kernels, local(): pl.pallas_call(attend_kernel, out_shape=jax.ShapeDtypeStruct((nctx, nrow...  1.95 us
    pallas_call x1, Pallas kernels, local(): pl.pallas_call(query_kernel, out_shape=(half, half), in_specs=[HBM, HBM],...  1.26 us
    ppermute x1, waiting for transfers between devices, local(): swapped = lax.ppermute(send, 'ctx', [(i, i ^ 1) for i in range(nctx)])  1.16 us
  transfers between devices with their start and end apart: 2, of which 2 were waited for; matrix products, arithmetic and copies ran while one was open for 0% of the time, Pallas kernels for 6%

profile of v1, /device:TPU:4, one launch (start us, length us, event | category | flops | bytes accessed | tf_op | source)
XLA Modules:
  0.0 45.6 jit_solution(16319540687235307875)
XLA Ops:
  0.0 1.3 %query.1 = (f32[16,128]{1,0:T(8,128)S(1)}, f32[16,128]{1,0:T(8,128)S(1)}) custom-call(bf16[4,256]{1,0:T(4,128)(2,1)} %hidden_ref.1, bf16[256,1024]{1,0:T(8,128)(2,1)} %weight_ref.2), custom_call_target="tpu_custom_call" | custom-call | tf_op jit(solution)/shard_map/query/pallas_call | solution.py:263
  1.3 0.1 collective-permute-start
  1.4 1.2 %collective-permute-done.swapped_ref.after_ref = f32[16,128]{1,0:T(8,128)S(1)} collective-permute-done((f32[16,128]{1,0:T(8,128)S(1)}, f32[16,128]{1,0:T(8,128)S(1)}, u32[]{:S(2)}, u32[]{:S(2)}) %collective-permute-start) | collective-permute-done | bytes 8224 | tf_op jit(solution)/shard_map/ppermute | solution.py:278
  2.5 0.7 %spread.1 = f32[32,16,128]{2,1,0:T(8,128)} custom-call(f32[16,128]{1,0:T(8,128)S(1)} %get-tuple-element.10.keep_ref, f32[16,128]{1,0:T(8,128)S(1)} %collective-permute-done.swapped_ref.after_ref), custom_call_target="tpu_custom_call" | custom-call | tf_op jit(solution)/shard_map/spread/pallas_call | solution.py:279
  3.2 6.5 %all-to-all-start = ((f32[32,16,128]{2,1,0:T(8,128)}), f32[32,16,128]{2,1,0:T(8,128)S(1)}, u32[]{:S(2)}, u32[]{:S(2)}) async-start(f32[32,16,128]{2,1,0:T(8,128)} %spread.1), calls=%async_computation | async-start | bytes 524288 | tf_op jit(solution)/shard_map/all_to_all | solution.py:287
  9.8 2.8 %fetch.1 = (bf16[8,512,128]{2,1,0:T(8,128)(2,1)S(1)}, bf16[8,512,128]{2,1,0:T(8,128)(2,1)S(1)}, s32[56]{0:T(128)S(1)}) custom-call(s32[4,1,16]{2,1,0:T(1,128)} %chosen_ref.1, s32[768]{0:T(1024)} %owner_ref.1, bf16[24,512,128]{2,1,0:T(8,128)(2,1)} %key_all.1, bf16[24,512,128]{2,1,0:T(8,128)(2,1)} %value_all.1, ...), custom_call_target="tpu_custom_call" | custom-call | bytes 8388608 | tf_op jit(solution)/shard_map/fetch/pallas_call | solution.py:290
  12.5 3.6 %all-to-all-done.parts_ref = f32[32,16,128]{2,1,0:T(8,128)S(1)} async-done(((f32[32,16,128]{2,1,0:T(8,128)}), f32[32,16,128]{2,1,0:T(8,128)S(1)}, u32[]{:S(2)}, u32[]{:S(2)}) %all-to-all-start) | async-done | bytes 262176 | tf_op jit(solution)/shard_map/all_to_all | solution.py:287
  16.1 0.0 copy-start
  16.1 2.0 %attend.1 = bf16[32,48,128]{2,1,0:T(8,128)(2,1)S(1)} custom-call(f32[32,16,128]{2,1,0:T(8,128)S(1)} %all-to-all-done.parts_ref, s32[56]{0:T(128)S(1)} %get-tuple-element.12.items_ref, bf16[8,512,128]{2,1,0:T(8,128)(2,1)S(1)} %get-tuple-element.13.key_ref, bf16[8,512,128]{2,1,0:T(8,128)(2,1)S(1)} %get-tuple-element.14.value_ref, ...), custom_call_target="tpu_custom_call" | custom-call | tf_op jit(solution)/shard_map/attend/pallas_call | solution.py:306
  18.1 13.8 %all_to_all.15.parts_ref = bf16[32,48,128]{2,1,0:T(8,128)(2,1)S(1)} all-to-all(bf16[32,48,128]{2,1,0:T(8,128)(2,1)S(1)} %attend.1), channel_id=1, replica_groups={{168,160,0,8,16,24,32,40,48,56,64,72,80,88,96,104,112,120,128,136,144,1..., dimensions={0} | all-to-all | bytes 786432 | tf_op jit(solution)/shard_map/all_to_all | solution.py:321
  31.9 0.0 copy-done
  31.9 0.6 %project.1 = f32[8,4,128]{2,1,0:T(4,128)S(1)} custom-call(bf16[32,48,128]{2,1,0:T(8,128)(2,1)S(1)} %all_to_all.15.parts_ref, bf16[1024,256]{1,0:T(8,128)(2,1)S(1)} %copy-done), custom_call_target="tpu_custom_call" | custom-call | tf_op jit(solution)/shard_map/project/pallas_call | solution.py:322
  32.5 12.5 %all_to_all.16.terms_ref = f32[8,4,128]{2,1,0:T(4,128)S(1)} all-to-all(f32[8,4,128]{2,1,0:T(4,128)S(1)} %project.1), channel_id=1, replica_groups={{4,5,6,7,0,1,2,3},{12,13,14,15,8,9,10,11},{20,21,22,23,16,17,18,19},{28..., dimensions={0} | all-to-all | bytes 32768 | tf_op jit(solution)/shard_map/all_to_all | solution.py:331
  45.0 0.6 %sum.1 = bf16[4,32]{1,0:T(4,128)(2,1)} custom-call(f32[8,4,128]{2,1,0:T(4,128)S(1)} %all_to_all.16.terms_ref), custom_call_target="tpu_custom_call" | custom-call | tf_op jit(solution)/shard_map/sum/pallas_call | solution.py:332
Async XLA Ops:
  1.3 1.3 %collective-permute-start = (f32[16,128]{1,0:T(8,128)S(1)}, f32[16,128]{1,0:T(8,128)S(1)}, u32[]{:S(2)}, u32[]{:S(2)}) collective-permute-start(f32[16,128]{1,0:T(8,128)S(1)} %get-tuple-element.11), channel_id=1, source_target_pairs={{0,8},{8,0},{16,24},{24,16},{32,40},{40,32},{48,56},{56,48},{64,72... | collective-permute-start | bytes 24584 | tf_op jit(solution)/shard_map/ppermute | solution.py:278
  3.2 12.9 %all-to-all-start = ((f32[32,16,128]{2,1,0:T(8,128)}), f32[32,16,128]{2,1,0:T(8,128)S(1)}, u32[]{:S(2)}, u32[]{:S(2)}) async-start(f32[32,16,128]{2,1,0:T(8,128)} %spread.1), calls=%async_computation | async-start | bytes 524288 | tf_op jit(solution)/shard_map/all_to_all | solution.py:287
  16.1 15.8 %copy-start = (bf16[1024,256]{1,0:T(8,128)(2,1)S(1)}, bf16[1024,256]{1,0:T(8,128)(2,1)}, u32[]{:S(2)}) copy-start(bf16[1024,256]{1,0:T(8,128)(2,1)} %weight_ref.3) | copy-start | bytes 1572868

commit v2 on v1

v2 whole, which is shorter than its diff:
```python
import functools

import jax
import jax.numpy as jnp
from jax import lax
from jax.experimental import pallas as pl
from jax.experimental.pallas import tpu as pltpu
from jax.sharding import PartitionSpec as P

QPK = 8
HD = 128
NEG = -1e30
VMEM = pl.BlockSpec(memory_space=pltpu.VMEM)
SMEM = pl.BlockSpec(memory_space=pltpu.SMEM)
HBM = pl.BlockSpec(memory_space=pltpu.HBM)
LIMIT = 24 * 1024 * 1024
GROUP = 4
AHEAD = 8
QSCALE = 256.0
STEP, STEPS = 12, 10
SPAN = 32
CTX_FIRST = 21
KVH_FIRST = 4
STRIPE_FIRST = (10, 14)


def in_hbm(array):
    return pltpu.with_memory_space_constraint(array, pltpu.HBM)


def find_items(chosen, owner, items, slots_here):
    nreq, _, topb = chosen.shape
    nblk = owner.shape[0] // nreq
    first = lax.axis_index("ctx") * slots_here
    for i in range(SPAN):
        items[i] = 0
    count = jnp.int32(0)
    for r in range(nreq):
        found = [owner[r * nblk + chosen[r, 0, j]] - first for j in range(topb)]
        for slot in found:
            items[count] = r
            items[SPAN + count] = slot
            count = count + ((slot >= 0) & (slot < slots_here)).astype(jnp.int32)
    items[2 * SPAN] = count


def query_kernel(
    slots_here, hidden_ref, weight_ref, chosen_ref, owner_ref, out_ref, items_ref,
    hidden, weight, chosen, owner, rows_ref, sems,
):
    tables = (
        pltpu.make_async_copy(chosen_ref, chosen, sems.at[0]),
        pltpu.make_async_copy(owner_ref, owner, sems.at[1]),
    )
    arrays = (
        pltpu.make_async_copy(hidden_ref, hidden, sems.at[2]),
        pltpu.make_async_copy(weight_ref, weight, sems.at[3]),
    )
    for copy in (*tables, *arrays):
        copy.start()
    for copy in tables:
        copy.wait()
    find_items(chosen, owner, items_ref, slots_here)
    for copy in arrays:
        copy.wait()
    part = jnp.dot(hidden[...], weight[...], preferred_element_type=jnp.float32)
    nreq = part.shape[0]
    for g in range(QPK):
        rows_ref[pl.ds(g, nreq, stride=QPK), :] = part[:, g * HD : (g + 1) * HD]
    out_ref[...] = rows_ref[...]


def fetch_kernel(items_ref, key_ref, value_ref, key_buf, value_buf, key_sem, value_sem):
    ahead = key_buf.shape[0]
    count = jnp.minimum(items_ref[2 * SPAN], ahead)

    def copies(place):
        slot = items_ref[SPAN + place]
        return (
            pltpu.make_async_copy(key_ref.at[slot], key_buf.at[place], key_sem.at[place]),
            pltpu.make_async_copy(value_ref.at[slot], value_buf.at[place], value_sem.at[place]),
        )

    def bring(i, carry):
        for copy in copies(i):
            copy.start()
        return carry

    def arrive(i, carry):
        for copy in copies(i):
            copy.wait()
        return carry

    lax.fori_loop(0, count, bring, 0)
    lax.fori_loop(0, count, arrive, 0)


def attend_kernel(
    query_ref, items_ref, key_ref, value_ref, key_all, value_all, out_ref,
    top_ref, total_ref, acc_ref, key_late, value_late, key_sem, value_sem,
):
    ahead = key_ref.shape[0]
    count = items_ref[2 * SPAN]

    def copies(i):
        place, slot = i - ahead, items_ref[SPAN + i]
        return (
            pltpu.make_async_copy(key_all.at[slot], key_late.at[place], key_sem.at[place]),
            pltpu.make_async_copy(value_all.at[slot], value_late.at[place], value_sem.at[place]),
        )

    def bring(i, carry):
        for copy in copies(i):
            copy.start()
        return carry

    def arrive(i, carry):
        for copy in copies(i):
            copy.wait()
        return carry

    lax.fori_loop(ahead, count, bring, 0)
    top_ref[...] = jnp.full(top_ref.shape, NEG, jnp.float32)
    total_ref[...] = jnp.zeros(total_ref.shape, jnp.float32)
    acc_ref[...] = jnp.zeros(acc_ref.shape, jnp.float32)

    def visit(step, keys, values, base, group):
        places = [step * group + u for u in range(group)]
        rows = [
            pl.ds(pl.multiple_of(items_ref[base + p] * QPK, QPK), QPK) for p in places
        ]
        scores = [
            lax.dot_general(
                query_ref[at, :].astype(jnp.bfloat16), keys[p], (((1,), (1,)), ((), ())),
                preferred_element_type=jnp.float32,
            ) * (1.0 / HD**0.5)
            for at, p in zip(rows, places)
        ]
        peaks = [jnp.max(x, axis=1, keepdims=True) for x in scores]
        expos = [jnp.exp(x - peak) for x, peak in zip(scores, peaks)]
        outs = [
            jnp.dot(x.astype(jnp.bfloat16), values[p], preferred_element_type=jnp.float32)
            for x, p in zip(expos, places)
        ]
        totals = [jnp.sum(x, axis=1, keepdims=True) for x in expos]
        found = [
            (base + p < count, *rest) for p, *rest in zip(places, rows, peaks, totals, outs)
        ]
        for here, rows, peak, total, out in found:
            peak = jnp.where(here, peak, NEG)
            old = top_ref[rows, :]
            new = jnp.maximum(old, peak)
            keep = jnp.exp(old - new)
            add = jnp.where(here, jnp.exp(peak - new), 0.0)
            top_ref[rows, :] = new
            total_ref[rows, :] = total_ref[rows, :] * keep + jnp.where(here, total, 0.0) * add
            acc_ref[rows, :] = acc_ref[rows, :] * keep + jnp.where(here, out, 0.0) * add

    @pl.when((count > 0) & (count <= GROUP))
    def _():
        visit(0, key_ref, value_ref, 0, GROUP)

    @pl.when(count > GROUP)
    def _():
        visit(0, key_ref, value_ref, 0, ahead)

    lax.fori_loop(ahead, count, arrive, 0)

    def visit_late(step, carry):
        visit(step, key_late, value_late, ahead, GROUP)
        return carry

    lax.fori_loop(0, jnp.maximum(count - ahead + GROUP - 1, 0) // GROUP, visit_late, 0)

    total = total_ref[...]
    some = total > 0.0
    safe = jnp.where(some, total, 1.0)
    out_ref[0] = acc_ref[...] / safe
    out_ref[1] = jnp.where(some, top_ref[...] + jnp.log(safe), NEG)


def join_kernel(own_ref, other_ref, out_ref):
    level_a, level_b = own_ref[1], other_ref[1]
    top = jnp.maximum(level_a, level_b)
    share_a, share_b = jnp.exp(level_a - top), jnp.exp(level_b - top)
    total = share_a + share_b
    mean = (share_a * own_ref[0] + share_b * other_ref[0]) / total
    level = top + jnp.log(total)
    most = jnp.max(jnp.max(jnp.abs(mean), axis=1, keepdims=True), axis=0, keepdims=True)
    ups = jnp.full((1, 1), 1.0, jnp.float32)
    downs = jnp.zeros(level.shape, jnp.float32)
    for i in range(STEPS):
        if i < STEPS - 1:
            ups = ups + jnp.where(most < 2.0 ** (3 - STEP * (i + 1)), 1.0, 0.0)
        downs = downs + jnp.where(jnp.abs(level) >= 2.0 ** (15 + STEP * i), 1.0, 0.0)
    mean = mean * scale_of(ups, STEP)
    level = level * scale_of(downs, -STEP)
    high = level.astype(jnp.bfloat16).astype(jnp.float32)
    middle = (level - high).astype(jnp.bfloat16).astype(jnp.float32)
    low = level - high - middle
    nrow = level.shape[0]
    lane = lax.broadcasted_iota(jnp.int32, level.shape, 1)
    row = lax.broadcasted_iota(jnp.int32, level.shape, 0)
    packed, counts = jnp.zeros(level.shape, jnp.float32), jnp.zeros(level.shape, jnp.float32)
    for i, part in enumerate((high, middle, low)):
        packed = jnp.where(lane == row + i * nrow, part, packed)
        counts = jnp.where(lane == row + i * nrow, downs, counts)
    packed = jnp.sum(packed, axis=0, keepdims=True)
    counts = jnp.sum(counts, axis=0, keepdims=True)
    out_ref[:nrow, :] = mean
    rest = (out_ref.shape[0] - nrow, HD)
    line = lax.broadcasted_iota(jnp.int32, rest, 0)
    out_ref[nrow:, :] = jnp.where(
        line == 0, packed, jnp.where(line == 1, counts, jnp.broadcast_to(ups, rest))
    )


def scale_of(count, step):
    scale = jnp.full(count.shape, 1.0, jnp.float32)
    for i in range(1, STEPS + 1):
        scale = jnp.where(count >= i, 2.0 ** (step * i), scale)
    return scale


def project_kernel(parts_ref, weight_ref, out_ref, rows_ref):
    ndev = parts_ref.shape[0]
    nrow = rows_ref.shape[0]
    lane = lax.broadcasted_iota(jnp.int32, (nrow, HD), 1)
    row = lax.broadcasted_iota(jnp.int32, (nrow, HD), 0)
    mine = (lane == row) | (lane == row + nrow) | (lane == row + 2 * nrow)
    levels, downs = [], []
    for d in range(ndev):
        rest = parts_ref[d, nrow:, :]
        packed = rest[0:1] * scale_of(rest[1:2], STEP)
        downs.append(scale_of(rest[2:3], -STEP))
        levels.append(jnp.sum(jnp.where(mine, packed, 0.0), axis=1, keepdims=True))
    top = functools.reduce(jnp.maximum, levels)
    total = jnp.zeros((nrow, 1), jnp.float32)
    acc = jnp.zeros((nrow, HD), jnp.float32)
    for d in range(ndev):
        share = jnp.exp(levels[d] - top)
        total = total + share
        acc = acc + share * (parts_ref[d, :nrow, :] * downs[d])
    rows_ref[...] = acc / total
    nreq = nrow // QPK
    term = jnp.zeros((nreq, weight_ref.shape[1]), jnp.float32)
    for g in range(QPK):
        heads = rows_ref[pl.ds(g, nreq, stride=QPK), :].astype(jnp.bfloat16)
        term = term + jnp.dot(
            heads, weight_ref[g * HD : (g + 1) * HD, :], preferred_element_type=jnp.float32
        )
    ndest = out_ref.shape[0]
    width = weight_ref.shape[1] // ndest
    for k in range(ndest):
        out_ref[(k - KVH_FIRST) % ndest, :, :width] = term[:, k * width : (k + 1) * width]


def planes(n, first):
    chips = [first // 2] + [i for i in range(n // 2) if i != first // 2]
    return [[2 * i + core for i in chips] for core in range(2)]


def stripes(n, firsts):
    groups = []
    for side, first in enumerate(firsts):
        chips = [first] + [i for i in range(n // 2) if i != first]
        groups.append([2 * i + (4 * i // n + side) % 2 for i in chips])
    return groups


def turned(n, first):
    return [[(first + i) % n for i in range(n)]]


def local(nctx, nkvh, hidden_in, w_query, key_cache, value_cache, chosen, owner_map, w_out):
    nreq = hidden_in.shape[0]
    nrow = nreq * QPK
    slots_here, block, _ = key_cache.shape
    params = pltpu.CompilerParams(vmem_limit_bytes=LIMIT)
    state = pltpu.VMEM((nrow, HD), jnp.float32)
    nchip = nctx // 2
    parts, items = pl.pallas_call(
        functools.partial(query_kernel, slots_here),
        out_shape=(
            jax.ShapeDtypeStruct((nrow, HD), jnp.float32),
            pltpu.SMEM((2 * SPAN + 8,), jnp.int32),
        ),
        in_specs=[HBM, HBM, HBM, HBM],
        out_specs=(VMEM, SMEM),
        scratch_shapes=[
            pltpu.VMEM(hidden_in.shape, hidden_in.dtype),
            pltpu.VMEM(w_query.shape, w_query.dtype),
            pltpu.SMEM(chosen.shape, jnp.int32),
            pltpu.SMEM(owner_map.shape, jnp.int32),
            state,
            pltpu.SemaphoreType.DMA((4,)),
        ],
        compiler_params=params,
        name="query",
    )(in_hbm(hidden_in), in_hbm(w_query), in_hbm(chosen), in_hbm(owner_map))
    swap = [(i, i ^ 1) for i in range(nctx)]
    other = lax.ppermute(parts, "ctx", swap)
    blocks = pltpu.VMEM((AHEAD, block, HD), key_cache.dtype)
    late = slots_here - AHEAD
    assert slots_here < SPAN
    keys, values = pl.pallas_call(
        fetch_kernel,
        out_shape=(blocks, blocks),
        in_specs=[SMEM, HBM, HBM],
        out_specs=(VMEM, VMEM),
        scratch_shapes=[
            pltpu.SemaphoreType.DMA((AHEAD,)),
            pltpu.SemaphoreType.DMA((AHEAD,)),
        ],
        compiler_params=params,
        cost_estimate=pl.CostEstimate(flops=0, transcendentals=0, bytes_accessed=4 << 20),
        name="fetch",
    )(items, in_hbm(key_cache), in_hbm(value_cache))
    other, keys, values = lax.optimization_barrier((other, keys, values))
    pair = ((parts + other) * QSCALE).astype(jnp.float16)
    every = jnp.broadcast_to(pair[None], (nchip, nrow, HD))
    every = lax.all_to_all(every, "ctx", 0, 0, tiled=True, axis_index_groups=stripes(nctx, STRIPE_FIRST))
    query = jnp.sum(every.astype(jnp.float32), axis=0) * (1.0 / QSCALE)
    states = pl.pallas_call(
        attend_kernel,
        out_shape=jax.ShapeDtypeStruct((2, nrow, HD), jnp.float32),
        in_specs=[VMEM, SMEM, VMEM, VMEM, HBM, HBM],
        out_specs=VMEM,
        scratch_shapes=[
            state, state, state,
            pltpu.VMEM((late, block, HD), key_cache.dtype),
            pltpu.VMEM((late, block, HD), key_cache.dtype),
            pltpu.SemaphoreType.DMA((late,)),
            pltpu.SemaphoreType.DMA((late,)),
        ],
        compiler_params=params,
        name="attend",
    )(query, items, keys, values, in_hbm(key_cache), in_hbm(value_cache))
    others = lax.ppermute(states, "ctx", swap)
    means = pl.pallas_call(
        join_kernel,
        out_shape=jax.ShapeDtypeStruct((nrow + 8, HD), jnp.float32),
        in_specs=[VMEM, VMEM],
        out_specs=VMEM,
        compiler_params=params,
        name="join",
    )(states, others)
    means = jnp.broadcast_to(means.astype(jnp.float16)[None], (nchip, *means.shape))
    means = lax.all_to_all(means, "ctx", 0, 0, tiled=True, axis_index_groups=planes(nctx, CTX_FIRST))
    means = means.astype(jnp.float32)
    terms = pl.pallas_call(
        project_kernel,
        out_shape=jax.ShapeDtypeStruct((nkvh, nreq, HD), jnp.float32),
        in_specs=[VMEM, VMEM],
        out_specs=VMEM,
        scratch_shapes=[state],
        compiler_params=params,
        name="project",
    )(means, w_out)
    terms = lax.all_to_all(terms, "kvh", 0, 0, tiled=True, axis_index_groups=turned(nkvh, KVH_FIRST))
    return jnp.sum(terms, axis=0)[:, : w_out.shape[1] // nkvh].astype(jnp.bfloat16)


def solution(mesh):
    placed = (
        P(None, "ctx"),
        P("ctx", "kvh"),
        P("ctx", None, "kvh"),
        P("ctx", None, "kvh"),
        P(None, "kvh", None),
        P(),
        P("kvh", "ctx"),
    )
    return jax.shard_map(
        functools.partial(local, mesh.shape["ctx"], mesh.shape["kvh"]),
        mesh=mesh, in_specs=placed, out_specs=P(None, ("ctx", "kvh")), check_vma=False,
    )
```

time: 45.9 us -> 41.2 us (0.90)
  blocking collectives: 26.3 us -> 35 us
  starting transfers between devices: 6.61 us -> 0.19 us
  Pallas kernels: 7.84 us -> 3.76 us
  waiting for transfers between devices: 4.75 us -> 1.23 us
  other arithmetic: 0 us -> 0.64 us
    all_to_all x1 -> x2, blocking collectives: 13.8 us -> 22.4 us  [the longest x1 11.9 us: local(): lax.all_to_all(every, 'ctx', 0, 0, tiled=True, axis_index_groups=stripes(...]
    all_to_all x1 -> x0, starting transfers between devices: 6.52 us -> none  [local(): lax.all_to_all(parts, 'ctx', 0, 0, tiled=True, axis_index_groups=order(nc...]
    pallas_call x5 -> x4, Pallas kernels: 7.27 us -> 3.3 us  [the longest x1 1.28 us: local(): pl.pallas_call(functools.partial(query_kernel, slots_here), out_shape=(ja...]
    all_to_all x1 -> x0, waiting for transfers between devices: 3.59 us -> none  [local(): lax.all_to_all(parts, 'ctx', 0, 0, tiled=True, axis_index_groups=order(nc...]
    reduce_sum x0 -> x2, other arithmetic: none -> 0.6 us  [the longest x1 0.58 us: local(): jnp.sum(terms, axis=0)[:, :w_out.shape[1] // nkvh].astype(jnp.bfloat16)]
    ppermute x1 -> x2, waiting for transfers between devices: 1.16 us -> 1.23 us  [the longest x1 1.19 us: local(): others = lax.ppermute(states, 'ctx', swap)]
  transfers between devices with their start and end apart: 2 -> 2, of which waited for: 2 -> 1; matrix products, arithmetic and copies ran while one was open for 0% -> 0% of each run, Pallas kernels for 6% -> 3%
where the time goes in v2:
time: 41.2 us; the launch traced here: 41 us
  blocking collectives  35 us (85%)
  Pallas kernels  3.76 us (9%)
  waiting for transfers between devices  1.23 us (3%)
  other arithmetic  0.64 us (2%)
    all_to_all x1, blocking collectives, local(): lax.all_to_all(terms, 'kvh', 0, 0, tiled=True, axis_index_groups=turned(n...  12.6 us
    all_to_all x1, blocking collectives, local(): lax.all_to_all(every, 'ctx', 0, 0, tiled=True, axis_index_groups=stripes(...  11.9 us
    all_to_all x1, blocking collectives, local(): lax.all_to_all(means, 'ctx', 0, 0, tiled=True, axis_index_groups=planes(n...  10.5 us
    pallas_call x1, Pallas kernels, local(): pl.pallas_call(functools.partial(query_kernel, slots_here), out_shape=(ja...  1.28 us
    ppermute x1, waiting for transfers between devices, local(): others = lax.ppermute(states, 'ctx', swap)  1.19 us
    pallas_call x1, Pallas kernels, local(): pl.pallas_call(fetch_kernel, out_shape=(blocks, blocks), in_specs=[SMEM,...  1.12 us
  transfers between devices with their start and end apart: 2, of which 1 were waited for; matrix products, arithmetic and copies ran while one was open for 0% of the time, Pallas kernels for 3%

profile of v2, /device:TPU:4, one launch (start us, length us, event | category | flops | bytes accessed | tf_op | source)
XLA Modules:
  0.0 41.0 jit_solution(11596548676556891027)
XLA Ops:
  0.0 1.3 %query.1 = (f32[32,128]{1,0:T(8,128)S(1)}, s32[72]{0:T(128)S(4)}) custom-call(bf16[4,256]{1,0:T(4,128)(2,1)} %hidden_ref.1, bf16[256,1024]{1,0:T(8,128)(2,1)} %weight_ref.2, s32[4,1,16]{2,1,0:T(1,128)} %chosen_ref.1, s32[768]{0:T(1024)} %owner_ref.1), custom_call_target="tpu_custom_call" | custom-call | tf_op jit(solution)/shard_map/query/pallas_call | solution.py:282
  1.3 0.1 collective-permute-start
  1.4 1.1 %fetch.1 = (bf16[8,512,128]{2,1,0:T(8,128)(2,1)S(1)}, bf16[8,512,128]{2,1,0:T(8,128)(2,1)S(1)}) custom-call(s32[72]{0:T(128)S(4)} %get-tuple-element.13.items_ref, bf16[24,512,128]{2,1,0:T(8,128)(2,1)} %key_all.1, bf16[24,512,128]{2,1,0:T(8,128)(2,1)} %value_all.1), custom_call_target="tpu_custom_call" | custom-call | bytes 4194304 | tf_op jit(solution)/shard_map/fetch/pallas_call | solution.py:306
  2.5 0.0 collective-permute-done
  2.6 11.9 %all_to_all.15 = f16[16,32,128]{2,1,0:T(8,128)(2,1)S(1)} all-to-all(f16[16,32,128]{2,1,0:T(8,128)(2,1)S(1)} %broadcast_in_dim.4), channel_id=1, replica_groups={{168,0,16,32,48,64,80,96,112,136,152,184,200,216,232,248},{224,8,24,40,..., dimensions={0} | all-to-all | bytes 262144 | tf_op jit(solution)/shard_map/all_to_all | solution.py:322
  14.5 0.0 copy-start
  14.5 0.8 %attend.1.own_ref = f32[2,32,128]{2,1,0:T(8,128)S(1)} custom-call(f32[32,128]{1,0:T(8,128)S(1)} %broadcast_multiply_fusion.query_ref, s32[72]{0:T(128)S(4)} %get-tuple-element.13.items_ref, bf16[8,512,128]{2,1,0:T(8,128)(2,1)S(1)} %get-tuple-element.17.key_ref, bf16[8,512,128]{2,1,0:T(8,128)(2,1)S(1)} %get-tuple-element.18.value_ref, ...), custom_call_target="tpu_custom_call" | custom-call | tf_op jit(solution)/shard_map/attend/pallas_call | solution.py:324
  15.3 0.1 collective-permute-start.1
  15.4 1.2 %collective-permute-done.1.other_ref = f32[2,32,128]{2,1,0:T(8,128)S(1)} collective-permute-done((f32[2,32,128]{2,1,0:T(8,128)S(1)}, f32[2,32,128]{2,1,0:T(8,128)S(1)}, u32[]{:S(2)}, u32[]{:S(2)}) %collective-permute-start.1) | collective-permute-done | bytes 32800 | tf_op jit(solution)/shard_map/ppermute | solution.py:339
  16.6 0.1 join.1
  16.8 10.5 %all_to_all.16 = f16[16,40,128]{2,1,0:T(8,128)(2,1)S(1)} all-to-all(f16[16,40,128]{2,1,0:T(8,128)(2,1)S(1)} %broadcast_in_dim.5), channel_id=1, replica_groups={{160,0,16,32,48,64,80,96,112,128,144,176,192,208,224,240},{168,8,24,40,..., dimensions={0} | all-to-all | bytes 327680 | tf_op jit(solution)/shard_map/all_to_all | solution.py:349
  27.3 0.0 copy-done
  27.3 0.5 %project.1 = f32[8,4,128]{2,1,0:T(4,128)S(1)} custom-call(f32[16,40,128]{2,1,0:T(8,128)S(1)} %convert_element_type.16.parts_ref, bf16[1024,256]{1,0:T(8,128)(2,1)S(1)} %copy-done), custom_call_target="tpu_custom_call" | custom-call | tf_op jit(solution)/shard_map/project/pallas_call | solution.py:351
  27.8 12.6 %all_to_all.17 = f32[8,4,128]{2,1,0:T(4,128)S(1)} all-to-all(f32[8,4,128]{2,1,0:T(4,128)S(1)} %project.1), channel_id=1, replica_groups={{4,5,6,7,0,1,2,3},{12,13,14,15,8,9,10,11},{20,21,22,23,16,17,18,19},{28..., dimensions={0} | all-to-all | bytes 32768 | tf_op jit(solution)/shard_map/all_to_all | solution.py:360
  40.4 0.6 %reduce_sum.19 = bf16[4,128]{1,0:T(4,128)(2,1)} reduce(f32[8,4,128]{2,1,0:T(4,128)S(1)} %all_to_all.17, f32[]{:T(128)} %constant.1.clone.1), dimensions={0}, to_apply=%region_1.0 | reduce | flops 3584 | bytes 17412 | tf_op jit(solution)/shard_map/reduce_sum | solution.py:361
  (7 shorter events, 0.1 us)
Async XLA Ops:
  1.3 1.3 %collective-permute-start = (f32[32,128]{1,0:T(8,128)S(1)}, f32[32,128]{1,0:T(8,128)S(1)}, u32[]{:S(2)}, u32[]{:S(2)}) collective-permute-start(f32[32,128]{1,0:T(8,128)S(1)} %get-tuple-element.12), channel_id=1, source_target_pairs={{0,8},{8,0},{16,24},{24,16},{32,40},{40,32},{48,56},{56,48},{64,72... | collective-permute-start | bytes 49160 | tf_op jit(solution)/shard_map/ppermute | solution.py:302
  14.5 12.8 %copy-start = (bf16[1024,256]{1,0:T(8,128)(2,1)S(1)}, bf16[1024,256]{1,0:T(8,128)(2,1)}, u32[]{:S(2)}) copy-start(bf16[1024,256]{1,0:T(8,128)(2,1)} %weight_ref.3) | copy-start | bytes 1572868
  15.3 1.3 %collective-permute-start.1 = (f32[2,32,128]{2,1,0:T(8,128)S(1)}, f32[2,32,128]{2,1,0:T(8,128)S(1)}, u32[]{:S(2)}, u32[]{:S(2)}) collective-permute-start(f32[2,32,128]{2,1,0:T(8,128)S(1)} %attend.1.own_ref), channel_id=1, source_target_pairs={{0,8},{8,0},{16,24},{24,16},{32,40},{40,32},{48,56},{56,48},{64,72... | collective-permute-start | bytes 98312 | tf_op jit(solution)/shard_map/ppermute | solution.py:339

commit v3 on v2

--- a/solution.py
+++ b/solution.py
@@ -138,10 +138,15 @@
         ]
         peaks = [jnp.max(x, axis=1, keepdims=True) for x in scores]
         expos = [jnp.exp(x - peak) for x, peak in zip(scores, peaks)]
+        highs = [x.astype(jnp.bfloat16) for x in expos]
+        lows = [(x - h.astype(jnp.float32)).astype(jnp.bfloat16) for x, h in zip(expos, highs)]
         outs = [
-            jnp.dot(x.astype(jnp.bfloat16), values[p], preferred_element_type=jnp.float32)
-            for x, p in zip(expos, places)
+            jnp.dot(
+                jnp.concatenate([h, w], axis=0), values[p], preferred_element_type=jnp.float32
+            )
+            for h, w, p in zip(highs, lows, places)
         ]
+        outs = [x[:QPK] + x[QPK:] for x in outs]
         totals = [jnp.sum(x, axis=1, keepdims=True) for x in expos]
         found = [
             (base + p < count, *rest) for p, *rest in zip(places, rows, peaks, totals, outs)

time: 41.2 us -> 41.2 us (level)
  Pallas kernels: 3.76 us -> 2.36 us
  waiting for transfers between devices: 1.23 us -> 1.86 us
  starting transfers between devices: 0.19 us -> 0.61 us
    ppermute x1, waiting for transfers between devices: 0.04 us -> 1 us  [local(): other = lax.ppermute(parts, 'ctx', swap)]
    pallas_call x1, Pallas kernels: 1.12 us -> 0.16 us  [local(): pl.pallas_call(fetch_kernel, out_shape=(blocks, blocks), in_specs=[SMEM,...]
    all_to_all x1, blocking collectives: 10.5 us -> 11.2 us  [local(): lax.all_to_all(means, 'ctx', 0, 0, tiled=True, axis_index_groups=planes(n...]
    pallas_call x1, Pallas kernels: 0.77 us -> 0.34 us  [local(): pl.pallas_call(attend_kernel, out_shape=jax.ShapeDtypeStruct((2, nrow, HD...]
    ppermute x1, starting transfers between devices: 0.09 us -> 0.52 us  [local(): others = lax.ppermute(states, 'ctx', swap)]
  transfers between devices with their start and end apart: 2 -> 2, of which waited for: 1 -> 2; matrix products, arithmetic and copies ran while one was open for 0% -> 0% of each run, Pallas kernels for 3% -> 0%
where the time goes in v3:
time: 41.2 us; the launch traced here: 41.1 us
  blocking collectives  35.4 us (86%)
  Pallas kernels  2.36 us (6%)
  waiting for transfers between devices  1.86 us (5%)
  other arithmetic  0.64 us (2%)
  starting transfers between devices  0.61 us (1%)
    all_to_all x1, blocking collectives, local(): lax.all_to_all(terms, 'kvh', 0, 0, tiled=True, axis_index_groups=turned(n...  12.5 us
    all_to_all x1, blocking collectives, local(): lax.all_to_all(every, 'ctx', 0, 0, tiled=True, axis_index_groups=stripes(...  11.7 us
    all_to_all x1, blocking collectives, local(): lax.all_to_all(means, 'ctx', 0, 0, tiled=True, axis_index_groups=planes(n...  11.2 us
    pallas_call x1, Pallas kernels, local(): pl.pallas_call(functools.partial(query_kernel, slots_here), out_shape=(ja...  1.28 us
    ppermute x1, waiting for transfers between devices, local(): other = lax.ppermute(parts, 'ctx', swap)  1 us
    ppermute x1, waiting for transfers between devices, local(): others = lax.ppermute(states, 'ctx', swap)  0.86 us
  transfers between devices with their start and end apart: 2, of which 2 were waited for; matrix products, arithmetic and copies ran while one was open for 0% of the time, Pallas kernels for 0%

profile of v3, /device:TPU:4, one launch (start us, length us, event | category | flops | bytes accessed | tf_op | source)
XLA Modules:
  0.0 41.1 jit_solution(16972616297102035716)
XLA Ops:
  0.0 1.3 %query.1 = (f32[32,128]{1,0:T(8,128)S(1)}, s32[72]{0:T(128)S(4)}) custom-call(bf16[4,256]{1,0:T(4,128)(2,1)} %hidden_ref.1, bf16[256,1024]{1,0:T(8,128)(2,1)} %weight_ref.2, s32[4,1,16]{2,1,0:T(1,128)} %chosen_ref.1, s32[768]{0:T(1024)} %owner_ref.1), custom_call_target="tpu_custom_call" | custom-call | tf_op jit(solution)/shard_map/query/pallas_call | solution.py:287
  1.3 0.1 collective-permute-start
  1.4 0.2 fetch.1
  1.6 1.0 %collective-permute-done = f32[32,128]{1,0:T(8,128)S(1)} collective-permute-done((f32[32,128]{1,0:T(8,128)S(1)}, f32[32,128]{1,0:T(8,128)S(1)}, u32[]{:S(2)}, u32[]{:S(2)}) %collective-permute-start) | collective-permute-done | bytes 16416 | tf_op jit(solution)/shard_map/ppermute | solution.py:307
  2.6 11.7 %all_to_all.15 = f16[16,32,128]{2,1,0:T(8,128)(2,1)S(1)} all-to-all(f16[16,32,128]{2,1,0:T(8,128)(2,1)S(1)} %broadcast_in_dim.4), channel_id=1, replica_groups={{168,0,16,32,48,64,80,96,112,136,152,184,200,216,232,248},{224,8,24,40,..., dimensions={0} | all-to-all | bytes 262144 | tf_op jit(solution)/shard_map/all_to_all | solution.py:327
  14.4 0.0 copy-start
  14.4 0.3 attend.1.own_ref
  14.7 0.5 %collective-permute-start.1 = (f32[2,32,128]{2,1,0:T(8,128)S(1)}, f32[2,32,128]{2,1,0:T(8,128)S(1)}, u32[]{:S(2)}, u32[]{:S(2)}) collective-permute-start(f32[2,32,128]{2,1,0:T(8,128)S(1)} %attend.1.own_ref), channel_id=1, source_target_pairs={{0,8},{8,0},{16,24},{24,16},{32,40},{40,32},{48,56},{56,48},{64,72... | collective-permute-start | bytes 98312 | tf_op jit(solution)/shard_map/ppermute | solution.py:344
  15.2 0.9 %collective-permute-done.1.other_ref = f32[2,32,128]{2,1,0:T(8,128)S(1)} collective-permute-done((f32[2,32,128]{2,1,0:T(8,128)S(1)}, f32[2,32,128]{2,1,0:T(8,128)S(1)}, u32[]{:S(2)}, u32[]{:S(2)}) %collective-permute-start.1) | collective-permute-done | bytes 32800 | tf_op jit(solution)/shard_map/ppermute | solution.py:344
  16.1 0.1 join.1
  16.3 11.2 %all_to_all.16 = f16[16,40,128]{2,1,0:T(8,128)(2,1)S(1)} all-to-all(f16[16,40,128]{2,1,0:T(8,128)(2,1)S(1)} %broadcast_in_dim.5), channel_id=1, replica_groups={{160,0,16,32,48,64,80,96,112,128,144,176,192,208,224,240},{168,8,24,40,..., dimensions={0} | all-to-all | bytes 327680 | tf_op jit(solution)/shard_map/all_to_all | solution.py:354
  27.5 0.0 copy-done
  27.5 0.5 %project.1 = f32[8,4,128]{2,1,0:T(4,128)S(1)} custom-call(f32[16,40,128]{2,1,0:T(8,128)S(1)} %convert_element_type.16.parts_ref, bf16[1024,256]{1,0:T(8,128)(2,1)S(1)} %copy-done), custom_call_target="tpu_custom_call" | custom-call | tf_op jit(solution)/shard_map/project/pallas_call | solution.py:356
  28.0 12.5 %all_to_all.17 = f32[8,4,128]{2,1,0:T(4,128)S(1)} all-to-all(f32[8,4,128]{2,1,0:T(4,128)S(1)} %project.1), channel_id=1, replica_groups={{4,5,6,7,0,1,2,3},{12,13,14,15,8,9,10,11},{20,21,22,23,16,17,18,19},{28..., dimensions={0} | all-to-all | bytes 32768 | tf_op jit(solution)/shard_map/all_to_all | solution.py:365
  40.5 0.6 %reduce_sum.19 = bf16[4,128]{1,0:T(4,128)(2,1)} reduce(f32[8,4,128]{2,1,0:T(4,128)S(1)} %all_to_all.17, f32[]{:T(128)} %constant.1.clone.1), dimensions={0}, to_apply=%region_1.0 | reduce | flops 3584 | bytes 17412 | tf_op jit(solution)/shard_map/reduce_sum | solution.py:366
  (7 shorter events, 0.1 us)
Async XLA Ops:
  1.3 1.3 %collective-permute-start = (f32[32,128]{1,0:T(8,128)S(1)}, f32[32,128]{1,0:T(8,128)S(1)}, u32[]{:S(2)}, u32[]{:S(2)}) collective-permute-start(f32[32,128]{1,0:T(8,128)S(1)} %get-tuple-element.12), channel_id=1, source_target_pairs={{0,8},{8,0},{16,24},{24,16},{32,40},{40,32},{48,56},{56,48},{64,72... | collective-permute-start | bytes 49160 | tf_op jit(solution)/shard_map/ppermute | solution.py:307
  14.4 13.1 %copy-start = (bf16[1024,256]{1,0:T(8,128)(2,1)S(1)}, bf16[1024,256]{1,0:T(8,128)(2,1)}, u32[]{:S(2)}) copy-start(bf16[1024,256]{1,0:T(8,128)(2,1)} %weight_ref.3) | copy-start | bytes 1572868
  14.7 1.4 %collective-permute-start.1 = (f32[2,32,128]{2,1,0:T(8,128)S(1)}, f32[2,32,128]{2,1,0:T(8,128)S(1)}, u32[]{:S(2)}, u32[]{:S(2)}) collective-permute-start(f32[2,32,128]{2,1,0:T(8,128)S(1)} %attend.1.own_ref), channel_id=1, source_target_pairs={{0,8},{8,0},{16,24},{24,16},{32,40},{40,32},{48,56},{56,48},{64,72... | collective-permute-start | bytes 98312 | tf_op jit(solution)/shard_map/ppermute | solution.py:344

commit v4 on v2

--- a/solution.py
+++ b/solution.py
@@ -20,7 +20,7 @@
 STEP, STEPS = 12, 10
 SPAN = 32
 CTX_FIRST = 21
-KVH_FIRST = 4
+KVH_FIRST = 5
 STRIPE_FIRST = (10, 14)
 
 

time: 41.2 us -> 41.3 us (level)
  no operation moved by 1% of the time
where the time goes in v4:
time: 41.3 us; the launch traced here: 41.1 us
  blocking collectives  35 us (85%)
  Pallas kernels  3.89 us (9%)
  waiting for transfers between devices  1.2 us (3%)
  other arithmetic  0.65 us (2%)
    all_to_all x1, blocking collectives, local(): lax.all_to_all(terms, 'kvh', 0, 0, tiled=True, axis_index_groups=turned(n...  12.5 us
    all_to_all x1, blocking collectives, local(): lax.all_to_all(every, 'ctx', 0, 0, tiled=True, axis_index_groups=stripes(...  11.8 us
    all_to_all x1, blocking collectives, local(): lax.all_to_all(means, 'ctx', 0, 0, tiled=True, axis_index_groups=planes(n...  10.7 us
    pallas_call x1, Pallas kernels, local(): pl.pallas_call(functools.partial(query_kernel, slots_here), out_shape=(ja...  1.28 us
    pallas_call x1, Pallas kernels, local(): pl.pallas_call(fetch_kernel, out_shape=(blocks, blocks), in_specs=[SMEM,...  1.25 us
    ppermute x1, waiting for transfers between devices, local(): others = lax.ppermute(states, 'ctx', swap)  1.19 us
  transfers between devices with their start and end apart: 2, of which 1 were waited for; matrix products, arithmetic and copies ran while one was open for 0% of the time, Pallas kernels for 3%

profile of v4, /device:TPU:4, one launch (start us, length us, event | category | flops | bytes accessed | tf_op | source)
XLA Modules:
  0.0 41.1 jit_solution(15505268020451091333)
XLA Ops:
  0.0 1.3 %query.1 = (f32[32,128]{1,0:T(8,128)S(1)}, s32[72]{0:T(128)S(4)}) custom-call(bf16[4,256]{1,0:T(4,128)(2,1)} %hidden_ref.1, bf16[256,1024]{1,0:T(8,128)(2,1)} %weight_ref.2, s32[4,1,16]{2,1,0:T(1,128)} %chosen_ref.1, s32[768]{0:T(1024)} %owner_ref.1), custom_call_target="tpu_custom_call" | custom-call | tf_op jit(solution)/shard_map/query/pallas_call | solution.py:282
  1.3 0.1 collective-permute-start
  1.4 1.2 %fetch.1 = (bf16[8,512,128]{2,1,0:T(8,128)(2,1)S(1)}, bf16[8,512,128]{2,1,0:T(8,128)(2,1)S(1)}) custom-call(s32[72]{0:T(128)S(4)} %get-tuple-element.13.items_ref, bf16[24,512,128]{2,1,0:T(8,128)(2,1)} %key_all.1, bf16[24,512,128]{2,1,0:T(8,128)(2,1)} %value_all.1), custom_call_target="tpu_custom_call" | custom-call | bytes 4194304 | tf_op jit(solution)/shard_map/fetch/pallas_call | solution.py:306
  2.6 0.0 collective-permute-done
  2.7 11.8 %all_to_all.15 = f16[16,32,128]{2,1,0:T(8,128)(2,1)S(1)} all-to-all(f16[16,32,128]{2,1,0:T(8,128)(2,1)S(1)} %broadcast_in_dim.4), channel_id=1, replica_groups={{168,0,16,32,48,64,80,96,112,136,152,184,200,216,232,248},{224,8,24,40,..., dimensions={0} | all-to-all | bytes 262144 | tf_op jit(solution)/shard_map/all_to_all | solution.py:322
  14.5 0.0 copy-start
  14.6 0.8 %attend.1.own_ref = f32[2,32,128]{2,1,0:T(8,128)S(1)} custom-call(f32[32,128]{1,0:T(8,128)S(1)} %broadcast_multiply_fusion.query_ref, s32[72]{0:T(128)S(4)} %get-tuple-element.13.items_ref, bf16[8,512,128]{2,1,0:T(8,128)(2,1)S(1)} %get-tuple-element.17.key_ref, bf16[8,512,128]{2,1,0:T(8,128)(2,1)S(1)} %get-tuple-element.18.value_ref, ...), custom_call_target="tpu_custom_call" | custom-call | tf_op jit(solution)/shard_map/attend/pallas_call | solution.py:324
  15.3 0.1 collective-permute-start.1
  15.4 1.2 %collective-permute-done.1.other_ref = f32[2,32,128]{2,1,0:T(8,128)S(1)} collective-permute-done((f32[2,32,128]{2,1,0:T(8,128)S(1)}, f32[2,32,128]{2,1,0:T(8,128)S(1)}, u32[]{:S(2)}, u32[]{:S(2)}) %collective-permute-start.1) | collective-permute-done | bytes 32800 | tf_op jit(solution)/shard_map/ppermute | solution.py:339
  16.6 0.1 join.1
  16.8 10.7 %all_to_all.16 = f16[16,40,128]{2,1,0:T(8,128)(2,1)S(1)} all-to-all(f16[16,40,128]{2,1,0:T(8,128)(2,1)S(1)} %broadcast_in_dim.5), channel_id=1, replica_groups={{160,0,16,32,48,64,80,96,112,128,144,176,192,208,224,240},{168,8,24,40,..., dimensions={0} | all-to-all | bytes 327680 | tf_op jit(solution)/shard_map/all_to_all | solution.py:349
  27.6 0.0 copy-done
  27.6 0.5 %project.1 = f32[8,4,128]{2,1,0:T(4,128)S(1)} custom-call(f32[16,40,128]{2,1,0:T(8,128)S(1)} %convert_element_type.16.parts_ref, bf16[1024,256]{1,0:T(8,128)(2,1)S(1)} %copy-done), custom_call_target="tpu_custom_call" | custom-call | tf_op jit(solution)/shard_map/project/pallas_call | solution.py:351
  28.1 12.5 %all_to_all.17 = f32[8,4,128]{2,1,0:T(4,128)S(1)} all-to-all(f32[8,4,128]{2,1,0:T(4,128)S(1)} %project.1), channel_id=1, replica_groups={{5,6,7,0,1,2,3,4},{13,14,15,8,9,10,11,12},{21,22,23,16,17,18,19,20},{29..., dimensions={0} | all-to-all | bytes 32768 | tf_op jit(solution)/shard_map/all_to_all | solution.py:360
  40.6 0.6 %reduce_sum.19 = bf16[4,128]{1,0:T(4,128)(2,1)} reduce(f32[8,4,128]{2,1,0:T(4,128)S(1)} %all_to_all.17, f32[]{:T(128)} %constant.1.clone.1), dimensions={0}, to_apply=%region_1.0 | reduce | flops 3584 | bytes 17412 | tf_op jit(solution)/shard_map/reduce_sum | solution.py:361
  (7 shorter events, 0.1 us)
Async XLA Ops:
  1.3 1.4 %collective-permute-start = (f32[32,128]{1,0:T(8,128)S(1)}, f32[32,128]{1,0:T(8,128)S(1)}, u32[]{:S(2)}, u32[]{:S(2)}) collective-permute-start(f32[32,128]{1,0:T(8,128)S(1)} %get-tuple-element.12), channel_id=1, source_target_pairs={{0,8},{8,0},{16,24},{24,16},{32,40},{40,32},{48,56},{56,48},{64,72... | collective-permute-start | bytes 49160 | tf_op jit(solution)/shard_map/ppermute | solution.py:302
  14.5 13.0 %copy-start = (bf16[1024,256]{1,0:T(8,128)(2,1)S(1)}, bf16[1024,256]{1,0:T(8,128)(2,1)}, u32[]{:S(2)}) copy-start(bf16[1024,256]{1,0:T(8,128)(2,1)} %weight_ref.3) | copy-start | bytes 1572868
  15.3 1.3 %collective-permute-start.1 = (f32[2,32,128]{2,1,0:T(8,128)S(1)}, f32[2,32,128]{2,1,0:T(8,128)S(1)}, u32[]{:S(2)}, u32[]{:S(2)}) collective-permute-start(f32[2,32,128]{2,1,0:T(8,128)S(1)} %attend.1.own_ref), channel_id=1, source_target_pairs={{0,8},{8,0},{16,24},{24,16},{32,40},{40,32},{48,56},{56,48},{64,72... | collective-permute-start | bytes 98312 | tf_op jit(solution)/shard_map/ppermute | solution.py:339
